TPU v7x, 512 devices: a whole 4x4x16 slice. The times are simulated.
512 devices in a mesh: prow: 32 (over x, y, core), pcol: 16 (over z).
Axes of the slice: x: 4, y: 4, z: 16, core: 2. Of those that a mesh axis runs over, the one named last changes fastest.
Arguments:
- slab: float32 [32768, 4096], P('prow', 'pcol'), may hold values from -6 to 6
- panel: float32 [32768, 256], P('prow', 'pcol'), may hold values from -0.1875 to 0.1875
- pivots: int32 [256], replicated, may hold values from 256 to 32767, as said below
Outputs:
- result: float32 [32768, 4096], P('prow', 'pcol')
Inputs may be any that keep to these rules, and one draw needn't show every extreme that they name: `pivots`: 256 distinct rows, none among the first 256; at most 32 of them lie in the 1024 rows of one process row, and some process row holds exactly 32.
All inputs are finite; a program needn't handle non-finite values.
Results may differ from a plain program's by a relative error of at most 0.00005.
Values sent between devices are 32-bit elements; how exact they have to be, the bound alone decides.
A program may use at most 64 MiB of HBM per device.

v0:
```python
import jax
import jax.numpy as jnp
from jax import lax
from jax.sharding import PartitionSpec as P


def broadcast(value, axis, root):
    mine = lax.axis_index(axis) == root
    return lax.psum(jnp.where(mine, value, jnp.zeros_like(value)), axis)


def solve_block(diag_block, right_side):
    return jax.scipy.linalg.solve_triangular(diag_block, right_side, lower=True, unit_diagonal=True)


def local(slab, panel, pivots):
    row_count = slab.shape[0]
    panel_width = pivots.shape[0]
    row_index = lax.axis_index("prow")
    row_start = row_index * row_count
    held_here = pivots // row_count == row_index
    local_row = jnp.clip(pivots - row_start, 0, row_count - 1)
    picked = jnp.take(slab, local_row, axis=0)
    masked = jnp.where(held_here[:, None], picked, jnp.zeros_like(picked))
    leading, diag_piece = (
        broadcast(slab[:panel_width], "prow", 0),
        broadcast(panel[:panel_width], "prow", 0),
    )
    diag_block = lax.all_gather(diag_piece, "pcol", axis=1, tiled=True)
    pivot_rows = lax.psum(masked, "prow")
    upper_rows = solve_block(diag_block, pivot_rows)
    target_row = jnp.where(held_here, local_row, row_count)
    swapped = slab.at[target_row].set(leading, mode="drop")
    updated = swapped - jnp.dot(
        lax.all_gather(panel, "pcol", axis=1, tiled=True),
        upper_rows,
        precision=lax.Precision.HIGHEST,
        preferred_element_type=jnp.float32,
    )
    top_block = jnp.where(row_index == 0, upper_rows, updated[:panel_width])
    return updated.at[:panel_width].set(top_block)


def solution(mesh):
    return jax.shard_map(
        local,
        mesh=mesh,
        in_specs=(P("prow", "pcol"), P("prow", "pcol"), P()),
        out_specs=P("prow", "pcol"),
        check_vma=False,
    )
```

profile of v0, /device:TPU:32, one launch (start us, length us, event | category | flops | bytes accessed | tf_op | source)
XLA Modules:
  0.0 216.6 jit_solution(5361861571704352834)
XLA Ops:
  7.4 0.0 all-reduce.3.cloned.1.call-start
  7.4 1.2 copy.24
  8.6 0.0 copy-start.1
  8.6 0.7 copy-done.1
  9.3 1.0 gather_fusion
  10.3 0.7 slice_select_fusion.1
  11.0 0.8 select_select_fusion
  11.9 0.0 all-reduce.3.cloned.1.call-update
  11.9 0.0 all-gather.2.cloned.1.call-start
  11.9 0.5 all-gather.2.cloned.1.call-update
  12.5 0.7 slice_select_fusion.2
  13.2 128.4 %psum.22 = f32[256,16]{0,1:T(8,128)S(1)} all-reduce(f32[256,16]{0,1:T(8,128)S(1)} %slice_select_fusion.2), channel_id=1, replica_groups=mesh['prow'=32,'pcol'=16] {'prow'}, use_global_device_ids=true, to_apply=%region_2.3 | all-reduce | flops 4096 | bytes 32768 | tf_op jit(solution)/shard_map/psum | solution.py:9
  141.6 34.6 %all_gather.6 = f32[256,256]{0,1:T(8,128)S(1)} all-gather(f32[256,16]{0,1:T(8,128)S(1)} %psum.22), channel_id=1, replica_groups=mesh['prow'=32,'pcol'=16] {'pcol'}, dimensions={1}, use_global_device_ids=true | all-gather | bytes 278528 | tf_op jit(solution)/shard_map/all_gather | solution.py:29
  176.2 0.1 copy.8
  176.4 0.1 convert_add_fusion
  176.5 0.1 triangular_solve.72
  176.6 4.0 %while.2 = (s32[]{:T(128)}, f32[256,256]{1,0:T(8,128)S(1)}, s32[2,2]{1,0:T(2,128)S(1)}, f32[2,128,128]{2,1,0:T(8,128)S(1)}, s32[]{:T(128)}) while((s32[]{:T(128)}, f32[256,256]{1,0:T(8,128)S(1)}, s32[2,2]{1,0:T(2,128)S(1)}, f32[2,128,128]{2,1,0:T(8,128)S(1)}, s32[]{:T(128)}) %tuple.25), condition=%wide.while_cond.1, body=%wide.while_body.1.sunk | while | flops 2 | bytes 131181 | solution.py:13
  176.6 0.6 fusion.14
  177.2 1.3 bitcast_dynamic-update-slice_fusion.2
  178.6 0.6 fusion.14
  179.2 1.3 bitcast_dynamic-update-slice_fusion.2
  180.5 19.7 %custom-call.4 = f32[2,128,128]{1,2,0:T(8,128)S(1)} custom-call(f32[2,128,128]{2,1,0:T(8,128)S(1)} %get-tuple-element.24), custom_call_target="InvertDiagBlocksLowerTriangular" | custom-call | tf_op jit(solution)/shard_map/jit(_solve_triangular)/triangular_solve | solution.py:13
  200.2 0.0 all-reduce.3.cloned.1.call-done
  200.3 0.0 copy-start
  200.3 2.2 %scatter_fusion = f32[1024,256]{1,0:T(8,128)S(1)} fusion(f32[1024,256]{1,0:T(8,128)S(1)} %copy.24, s32[256]{0:T(256)S(1)} %get-tuple-element.37, f32[256,256]{1,0:T(8,128)} %get-tuple-element.33), kind=kCustom, calls=%fused_computation.1 | custom fusion | bytes 787456 | tf_op jit(solution)/shard_map/scatter | solution.py:33
  202.5 0.0 copy-done
  202.5 0.3 fusion.2
  202.8 0.3 convolution_subtract_fusion
  203.1 0.3 fusion.5
  203.4 0.0 all-gather.2.cloned.1.call-done
  203.5 4.0 %fusion = f32[1024,256]{1,0:T(8,128)} fusion(f32[1024,256]{1,0:T(8,128)S(1)} %scatter_fusion, f32[1024,256]{0,1:T(8,128)} %all-gather.2.cloned.1.call-done, f32[128,256]{1,0:T(8,128)S(1)} %fusion.5, f32[128,256]{1,0:T(8,128)S(1)} %fusion.2), kind=kOutput, calls=%fused_computation.5 | convolution fusion | flops 805634048 | bytes 3407872 | tf_op jit(solution)/shard_map/dot_general | solution.py:34
  207.5 1.7 fusion.1
  (8 shorter events, 0.1 us)
Async XLA Ops:
  7.4 192.9 %all-reduce.3.cloned.1.call-start = ((), (), s32[]{:S(2)}) async-start(), calls=%async_computation.1 | async-start | bytes 1048576 | tf_op jit(solution)/shard_map/psum | solution.py:9
  8.6 0.7 copy-start.1
  11.9 191.6 %all-gather.2.cloned.1.call-start = ((), (), s32[]{:S(2)}) async-start(), calls=%async_computation | async-start | bytes 1114112 | tf_op jit(solution)/shard_map/all_gather | solution.py:35
  200.3 2.3 %copy-start = (f32[256,256]{1,0:T(8,128)S(1)}, f32[256,256]{1,0:T(8,128)}, u32[]{:S(2)}) copy-start(f32[256,256]{1,0:T(8,128)} %get-tuple-element.34) | copy-start | bytes 786436
Sparse Core Ops, SparseCore 0:
  12.0 138.7 all-reduce.2
Sparse Core Ops, SparseCore 1:
  14.6 75.2 all-gather.1
where the time goes:
time: 217 us
  blocking collectives  163 us (75%)
  other arithmetic  23.8 us (11%)
  between operations  15 us (7%)
  local copies, waits for them, and re-layouts  9.24 us (4%)
  matrix products  4.89 us (2%)
    psum x1, blocking collectives, broadcast(): return lax.psum(jnp.where(mine, value, jnp.zeros_like(value)), axis)  128 us
    all_gather x1, blocking collectives, local(): diag_block = lax.all_gather(diag_piece, 'pcol', axis=1, tiled=True)  34.6 us
    another operation x4, other arithmetic, solve_block(): jax.scipy.linalg.solve_triangular(diag_block, right_side, lower=True, uni...  19.8 us
  transfers between devices with their start and end apart: 2, of which 0 were waited for; matrix products, arithmetic and copies ran while one was open for 13% of the time, Pallas kernels for 0%

commit v1 on v0

--- a/solution.py
+++ b/solution.py
@@ -6,7 +6,7 @@
 
 def broadcast(value, axis, root):
     mine = lax.axis_index(axis) == root
-    return lax.psum(jnp.where(mine, value, jnp.zeros_like(value)), axis)
+    return jnp.sum(lax.all_gather(jnp.where(mine, value, jnp.zeros_like(value)), axis), axis=0)
 
 
 def solve_block(diag_block, right_side):

time: 217 us -> 305 us (1.41)
  the two profiles are of different devices: /device:TPU:32 before, /device:TPU:2 now
where the time goes in v1:
time: 305 us
  waiting for transfers between devices  186 us (61%)
  blocking collectives  61.6 us (20%)
  other arithmetic  29.1 us (10%)
  between operations  13.2 us (4%)
  local copies, waits for them, and re-layouts  8.48 us (3%)
  matrix products  6.7 us (2%)
    all_gather x1, waiting for transfers between devices, broadcast(): lax.all_gather(jnp.where(mine, value, jnp.zeros_like(value)), axis)  69.4 us
    all_gather x1, waiting for transfers between devices, local(): lax.all_gather(panel, 'pcol', axis=1, tiled=True)  67.3 us
    psum x1, waiting for transfers between devices, local(): pivot_rows = lax.psum(masked, 'prow')  48.2 us
    all_gather x1, blocking collectives, local(): diag_block = lax.all_gather(diag_piece, 'pcol', axis=1, tiled=True)  34 us
    all_gather x1, blocking collectives, broadcast(): lax.all_gather(jnp.where(mine, value, jnp.zeros_like(value)), axis)  27.6 us
    another operation x4, other arithmetic, solve_block(): jax.scipy.linalg.solve_triangular(diag_block, right_side, lower=True, uni...  19.8 us
  transfers between devices with their start and end apart: 3, of which 3 were waited for; matrix products, arithmetic and copies ran while one was open for 11% of the time, Pallas kernels for 0%

profile of v1, /device:TPU:2, one launch (start us, length us, event | category | flops | bytes accessed | tf_op | source)
XLA Modules:
  0.0 304.9 jit_solution(4301074251310003794)
XLA Ops:
  6.5 0.0 all-reduce.2.cloned.1.call-start
  6.5 1.2 copy.21
  7.8 0.7 compare_and_fusion
  8.5 0.7 compare_select_fusion.1
  9.2 1.0 gather_fusion
  10.1 0.8 select_select_fusion
  11.0 0.0 all-reduce.2.cloned.1.call-update
  11.0 0.0 all-gather.7.cloned.1.call-start
  11.0 0.7 slice_select_fusion.1
  11.8 0.0 all-gather.7.cloned.1.call-update
  11.8 0.0 all-gather.5.cloned.1.call-start
  11.8 0.7 all-gather.5.cloned.1.call-update
  12.5 0.7 slice_select_fusion.2
  13.3 27.6 %all-gather.1 = f32[8192,16]{0,1:T(8,128)S(1)} all-gather(f32[256,16]{0,1:T(8,128)S(1)} %slice_select_fusion.2), channel_id=3, replica_groups=mesh['prow'=32,'pcol'=16] {'prow'}, dimensions={0}, use_global_device_ids=true | all-gather | bytes 540672 | tf_op jit(solution)/shard_map/all_gather | solution.py:9
  40.9 0.2 copy.8
  41.0 0.1 bitcast_reduce_fusion
  41.1 34.0 %all_gather.22 = f32[256,256]{0,1:T(8,128)S(1)} all-gather(f32[256,16]{0,1:T(8,128)S(1)} %bitcast_reduce_fusion), channel_id=1, replica_groups=mesh['prow'=32,'pcol'=16] {'pcol'}, dimensions={1}, use_global_device_ids=true | all-gather | bytes 278528 | tf_op jit(solution)/shard_map/all_gather | solution.py:29
  75.1 0.1 copy.5
  75.2 0.1 convert_add_fusion
  75.3 0.1 triangular_solve.72
  75.4 4.1 %while.2 = (s32[]{:T(128)}, f32[256,256]{1,0:T(8,128)S(1)}, s32[2,2]{1,0:T(2,128)S(1)}, f32[2,128,128]{2,1,0:T(8,128)S(1)}, s32[]{:T(128)}) while((s32[]{:T(128)}, f32[256,256]{1,0:T(8,128)S(1)}, s32[2,2]{1,0:T(2,128)S(1)}, f32[2,128,128]{2,1,0:T(8,128)S(1)}, s32[]{:T(128)}) %tuple.25), condition=%wide.while_cond.1, body=%wide.while_body.1.sunk | while | flops 2 | bytes 131181 | solution.py:13
  75.4 0.6 fusion.14
  76.1 1.4 bitcast_dynamic-update-slice_fusion.2
  77.5 0.6 fusion.14
  78.1 1.4 bitcast_dynamic-update-slice_fusion.2
  79.5 19.7 %custom-call.4 = f32[2,128,128]{1,2,0:T(8,128)S(1)} custom-call(f32[2,128,128]{2,1,0:T(8,128)S(1)} %get-tuple-element.24), custom_call_target="InvertDiagBlocksLowerTriangular" | custom-call | tf_op jit(solution)/shard_map/jit(_solve_triangular)/triangular_solve | solution.py:13
  99.2 48.2 %all-reduce.2.cloned.1.call-done = f32[256,256]{1,0:T(8,128)} async-done(((f32[256,256]{1,0:T(8,128)}), f32[256,256]{1,0:T(8,128)}) %all-reduce.2.cloned.1.call-update) | async-done | bytes 262160 | tf_op jit(solution)/shard_map/psum | solution.py:30
  147.5 1.2 fusion.2
  148.7 1.2 convolution_subtract_fusion
  149.9 0.3 fusion.5
  150.2 69.4 %all-gather.7.cloned.1.call-done = f32[8192,256]{1,0:T(8,128)} async-done(((f32[256,256]{1,0:T(8,128)}), f32[8192,256]{1,0:T(8,128)}) %all-gather.7.cloned.1.call-update) | async-done | bytes 8388624 | tf_op jit(solution)/shard_map/all_gather | solution.py:9
  219.6 3.9 %reduce_sum.18 = f32[256,256]{1,0:T(8,128)S(1)} reduce(f32[32,256,256]{2,1,0:T(8,128)} %bitcast.29, f32[]{:T(128)} %constant.78.clone.1), dimensions={0}, to_apply=%region_0.1 | reduce | flops 2031616 | bytes 8650756 | tf_op jit(solution)/shard_map/reduce_sum | solution.py:9
  223.5 1.8 scatter_fusion
  225.4 67.3 %all-gather.5.cloned.1.call-done = f32[1024,256]{0,1:T(8,128)} async-done(((f32[1024,16]{0,1:T(8,128)}), f32[1024,256]{0,1:T(8,128)}) %all-gather.5.cloned.1.call-update) | async-done | bytes 1048592 | tf_op jit(solution)/shard_map/all_gather | solution.py:35
  292.7 4.0 %fusion = f32[1024,256]{1,0:T(8,128)} fusion(f32[1024,256]{1,0:T(8,128)S(1)} %scatter_fusion, f32[1024,256]{0,1:T(8,128)} %all-gather.5.cloned.1.call-done, f32[128,256]{1,0:T(8,128)S(1)} %fusion.5, f32[128,256]{1,0:T(8,128)S(1)} %fusion.2), kind=kOutput, calls=%fused_computation.5 | convolution fusion | flops 805634048 | bytes 3407872 | tf_op jit(solution)/shard_map/dot_general | solution.py:34
  296.7 1.7 fusion.1
  (6 shorter events, 0.0 us)
Async XLA Ops:
  6.5 140.9 %all-reduce.2.cloned.1.call-start = ((), (), s32[]{:S(2)}) async-start(), calls=%async_computation | async-start | bytes 524288 | tf_op jit(solution)/shard_map/psum | solution.py:30
  11.0 208.6 %all-gather.7.cloned.1.call-start = ((), (), s32[]{:S(2)}) async-start(), calls=%async_computation.2 | async-start | bytes 8650752 | tf_op jit(solution)/shard_map/all_gather | solution.py:9
  11.8 280.9 %all-gather.5.cloned.1.call-start = ((), (), s32[]{:S(2)}) async-start(), calls=%async_computation.1 | async-start | bytes 1114112 | tf_op jit(solution)/shard_map/all_gather | solution.py:35
Sparse Core Ops, SparseCore 0:
  11.1 136.3 all-reduce.1
  151.1 68.5 all-gather.6
  221.9 70.7 all-gather.4

commit v2 on v0

--- a/solution.py
+++ b/solution.py
@@ -26,7 +26,9 @@
         broadcast(slab[:panel_width], "prow", 0),
         broadcast(panel[:panel_width], "prow", 0),
     )
-    diag_block = lax.all_gather(diag_piece, "pcol", axis=1, tiled=True)
+    diag_block = jnp.concatenate(
+        lax.all_to_all(jnp.stack([diag_piece] * lax.axis_size("pcol")), "pcol", 0, 0), axis=1
+    )
     pivot_rows = lax.psum(masked, "prow")
     upper_rows = solve_block(diag_block, pivot_rows)
     target_row = jnp.where(held_here, local_row, row_count)

time: 217 us -> 331 us (1.53)
  the two profiles are of different devices: /device:TPU:32 before, /device:TPU:1 now
where the time goes in v2:
time: 331 us; the launch traced here: 330 us
  waiting for transfers between devices  137 us (41%)
  blocking collectives  125 us (38%)
  other arithmetic  23.8 us (7%)
  between operations  15 us (5%)
  starting transfers between devices  14.2 us (4%)
  local copies, waits for them, and re-layouts  9.9 us (3%)
  matrix products  4.89 us (1%)
    psum x1, waiting for transfers between devices, broadcast(): return lax.psum(jnp.where(mine, value, jnp.zeros_like(value)), axis)  137 us
    psum x1, blocking collectives, broadcast(): return lax.psum(jnp.where(mine, value, jnp.zeros_like(value)), axis)  125 us
    another operation x4, other arithmetic, solve_block(): jax.scipy.linalg.solve_triangular(diag_block, right_side, lower=True, uni...  19.8 us
    all_to_all x1, starting transfers between devices, local(): lax.all_to_all(jnp.stack([diag_piece] * lax.axis_size('pcol')), 'pcol', 0...  14.2 us
  transfers between devices with their start and end apart: 3, of which 1 were waited for; matrix products, arithmetic and copies ran while one was open for 9% of the time, Pallas kernels for 0%

profile of v2, /device:TPU:1, one launch (start us, length us, event | category | flops | bytes accessed | tf_op | source)
XLA Modules:
  0.0 330.2 jit_solution(4737349659794616052)
XLA Ops:
  7.4 1.2 copy.22
  8.6 0.7 slice_select_fusion.2
  9.3 125.0 %psum.22 = f32[256,16]{0,1:T(8,128)S(1)} all-reduce(f32[256,16]{0,1:T(8,128)S(1)} %slice_select_fusion.2), channel_id=1, replica_groups=mesh['prow'=32,'pcol'=16] {'prow'}, use_global_device_ids=true, to_apply=%region_2.3 | all-reduce | flops 4096 | bytes 32768 | tf_op jit(solution)/shard_map/psum | solution.py:9
  134.3 0.7 stack.2
  135.0 14.2 %all-to-all-start = ((f32[16,256,16]{1,2,0:T(8,128)}), f32[16,256,16]{1,2,0:T(8,128)S(1)}, u32[]{:S(2)}, u32[]{:S(2)}) async-start(f32[16,256,16]{1,2,0:T(8,128)} %stack.2), calls=%async_computation | async-start | bytes 524288 | tf_op jit(solution)/shard_map/all_to_all | solution.py:30
  149.2 0.0 copy-start.1
  149.2 0.0 all-reduce.3.cloned.1.call-start
  149.2 0.6 copy-done.1
  149.9 0.7 slice_select_fusion.1
  150.6 1.0 gather_fusion
  151.6 0.9 select_select_fusion
  152.5 0.0 all-reduce.3.cloned.1.call-update
  152.5 0.0 all-gather.2.cloned.1.call-start
  152.5 0.5 all-gather.2.cloned.1.call-update
  153.1 136.8 %all-reduce.3.cloned.1.call-done = (f32[256,256]{1,0:T(8,128)}, f32[256,256]{1,0:T(8,128)}) async-done(((f32[256,256]{1,0:T(8,128)}, f32[256,256]{1,0:T(8,128)}), (f32[256,256]{1,0:T(8,128)}, f32[256,256]{1,0:T(8,128)})) %all-reduce.3.cloned.1.call-update) | async-done | bytes 524304 | tf_op jit(solution)/shard_map/psum | solution.py:9
  289.9 2.2 scatter_fusion
  292.1 0.0 all-to-all-done
  292.1 0.1 copy.6
  292.3 0.0 copy-start
  292.3 0.1 convert_add_fusion
  292.4 0.1 triangular_solve.72
  292.5 4.0 %while.2 = (s32[]{:T(128)}, f32[256,256]{1,0:T(8,128)S(1)}, s32[2,2]{1,0:T(2,128)S(1)}, f32[2,128,128]{2,1,0:T(8,128)S(1)}, s32[]{:T(128)}) while((s32[]{:T(128)}, f32[256,256]{1,0:T(8,128)S(1)}, s32[2,2]{1,0:T(2,128)S(1)}, f32[2,128,128]{2,1,0:T(8,128)S(1)}, s32[]{:T(128)}) %tuple.25), condition=%wide.while_cond.1, body=%wide.while_body.1.sunk | while | flops 2 | bytes 131181 | solution.py:13
  292.5 0.6 fusion.14
  293.1 1.4 bitcast_dynamic-update-slice_fusion.2
  294.5 0.6 fusion.14
  295.0 1.4 bitcast_dynamic-update-slice_fusion.2
  296.4 19.7 %custom-call.4 = f32[2,128,128]{1,2,0:T(8,128)S(1)} custom-call(f32[2,128,128]{2,1,0:T(8,128)S(1)} %get-tuple-element.24), custom_call_target="InvertDiagBlocksLowerTriangular" | custom-call | tf_op jit(solution)/shard_map/jit(_solve_triangular)/triangular_solve | solution.py:13
  316.1 0.0 copy-done
  316.1 0.3 fusion.2
  316.4 0.3 convolution_subtract_fusion
  316.7 0.3 fusion.5
  317.0 0.0 all-gather.2.cloned.1.call-done
  317.1 4.0 %fusion = f32[1024,256]{1,0:T(8,128)} fusion(f32[1024,256]{1,0:T(8,128)S(1)} %scatter_fusion, f32[1024,256]{0,1:T(8,128)} %all-gather.2.cloned.1.call-done, f32[128,256]{1,0:T(8,128)S(1)} %fusion.5, f32[128,256]{1,0:T(8,128)S(1)} %fusion.2), kind=kOutput, calls=%fused_computation.5 | convolution fusion | flops 805634048 | bytes 3407872 | tf_op jit(solution)/shard_map/dot_general | solution.py:36
  321.1 1.7 fusion.1
  (8 shorter events, 0.1 us)
Async XLA Ops:
  135.0 157.1 %all-to-all-start = ((f32[16,256,16]{1,2,0:T(8,128)}), f32[16,256,16]{1,2,0:T(8,128)S(1)}, u32[]{:S(2)}, u32[]{:S(2)}) async-start(f32[16,256,16]{1,2,0:T(8,128)} %stack.2), calls=%async_computation | async-start | bytes 524288 | tf_op jit(solution)/shard_map/all_to_all | solution.py:30
  149.2 0.7 copy-start.1
  149.2 140.7 %all-reduce.3.cloned.1.call-start = ((), (), s32[]{:S(2)}) async-start(), calls=%async_computation.2 | async-start | bytes 1048576 | tf_op jit(solution)/shard_map/psum | solution.py:9
  152.5 164.6 %all-gather.2.cloned.1.call-start = ((), (), s32[]{:S(2)}) async-start(), calls=%async_computation.1 | async-start | bytes 1114112 | tf_op jit(solution)/shard_map/all_gather | solution.py:37
  292.3 23.8 %copy-start = (f32[256,256]{1,0:T(8,128)S(1)}, f32[256,256]{1,0:T(8,128)}, u32[]{:S(2)}) copy-start(f32[256,256]{1,0:T(8,128)} %get-tuple-element.34) | copy-start | bytes 786436
Sparse Core Ops, SparseCore 0:
  153.2 136.5 all-reduce.2
Sparse Core Ops, SparseCore 1:
  155.2 63.1 all-gather.1
